TPU v7x, 32 devices: a whole 2x2x4 slice. The times are simulated.
32 devices in a mesh: grp: 2 (over y), row: 4 (over x, core), col: 4 (over z).
Axes of the slice: x: 2, y: 2, z: 4, core: 2. Of those that a mesh axis runs over, the one named last changes fastest.
Arguments:
- video: bfloat16 [514, 32, 512], P('grp', 'row', 'col'), parts along dimension 0, may hold values from -6 to 6, as said below
- filters: float32 [4, 2, 7, 7], replicated, may hold values from -0.875 to 0.875
- start_basis: float32 [256, 64], replicated, may hold values from -6 to 6
Outputs:
- basis: float32 [512, 64], P('grp'), parts along dimension 0
- modes: float32 [16, 128, 256], P(('grp', 'row'), 'col'), parts along dimension 0
There are 2 independent parts, one for each index of `grp`. A program takes and returns all parts, laid end to end along the dimension named above; an argument that names none is the same for every part. Nothing has to cross between parts.
Inputs may be any that keep to these rules, and one draw needn't show every extreme that they name: `video`: grey levels: a fixed texture plus a per-pixel oscillation in time.
All inputs are finite; a program needn't handle non-finite values.
Results may differ from a plain program's by a relative error of at most 0.0034.
Values may be sent and summed in bfloat16 or wider, within the bound.
No kernel may reach another device: no remote copies, remote signals or barrier semaphores. Data moves between devices by JAX's collectives and lax.ppermute only.
A program may use at most 64 MiB of HBM per device.

v0:
```python
import jax
import jax.numpy as jnp
from jax import lax
from jax.sharding import PartitionSpec as P

FRAMES = 256
MODES = 64
ORIENT = 4
TAPS = 7
SWEEPS = 2


def padded_2(array, sides, width):
    for axis, dim in sides:
        size, length = (lax.axis_size(axis), array.shape[dim])
        up = [(i, (i + 1) % size) for i in range(size - 1)]
        down = [(j, i) for i, j in up]
        last = lax.slice_in_dim(array, length - width, length, axis=dim)
        first = lax.slice_in_dim(array, 0, width, axis=dim)
        before = lax.ppermute(last, axis, up)
        after = lax.ppermute(first, axis, down)
        array = jnp.concatenate([before, array, after], axis=dim)
    return array


def orthonormal(stacked):
    inner = jnp.dot(stacked.T, stacked, precision=lax.Precision.HIGHEST)
    factor = jnp.linalg.cholesky(inner)
    return lax.linalg.triangular_solve(
        factor, stacked, left_side=False, lower=True, transpose_a=True
    )


def on_device(video, filters, start_basis):
    tile_rows = video.shape[1]
    tile_cols = video.shape[2]
    padded = padded_2(video, (("row", 1), ("col", 2)), 3)

    def orient(taps):
        kernels = taps.reshape(2, 1, TAPS, TAPS)
        lifted = padded.astype(jnp.float32)[:, None]
        response = lax.conv_general_dilated(
            lifted, kernels, (1, 1), "VALID", precision=lax.Precision.HIGHEST
        )
        real_part = response[:, 0]
        imag_part = response[:, 1]
        prod_real = real_part[1:] * real_part[:-1] + imag_part[1:] * imag_part[:-1]
        prod_imag = imag_part[1:] * real_part[:-1] - real_part[1:] * imag_part[:-1]
        motion = prod_imag / jnp.sqrt(prod_real * prod_real + prod_imag * prod_imag + 1.0)
        pooled = motion.reshape(FRAMES, tile_rows // 4, 4, tile_cols // 4, 4).mean(axis=(2, 4))
        return pooled.astype(jnp.bfloat16)

    stacked = lax.map(orient, filters)
    flat = jnp.transpose(stacked, (1, 0, 2, 3)).reshape(FRAMES, -1)
    devices_all = lax.axis_size("row") * lax.axis_size("col")
    npix_all = flat.shape[1] * devices_all
    basis_now = start_basis
    local_gram = jnp.dot(flat, flat.T, preferred_element_type=jnp.float32)
    gram = lax.psum(local_gram, ("row", "col")) / npix_all
    for sweep in range(SWEEPS):
        basis_now = orthonormal(jnp.dot(gram, basis_now, precision=lax.Precision.HIGHEST))
    projected = jnp.dot(basis_now.astype(jnp.bfloat16).T, flat, preferred_element_type=jnp.float32)
    fields = projected.reshape(MODES, ORIENT, tile_rows // 4, tile_cols // 4)
    modes = jnp.transpose(fields, (2, 3, 1, 0)).reshape(
        tile_rows // 4, tile_cols // 4, ORIENT * MODES
    )
    return (basis_now, modes)


def solution(mesh):
    return jax.shard_map(
        on_device,
        mesh=mesh,
        in_specs=(P("grp", "row", "col"), P(), P()),
        out_specs=(P("grp", None), P(("grp", "row"), "col", None)),
        check_vma=False,
    )
```

profile of v0, /device:TPU:1, one launch (start us, length us, event | category | flops | bytes accessed | tf_op | source)
XLA Modules:
  0.0 571.4 jit_solution(12141925055525839283)
XLA Ops:
  7.2 1.5 copy.25
  8.8 4.5 collective-permute-start
  13.3 1.9 collective-permute-start.1
  15.2 1.7 collective-permute-done
  16.9 4.4 collective-permute-done.1
  21.4 3.2 collective-permute-start.2
  24.6 1.3 collective-permute-start.3
  25.9 3.4 collective-permute-done.3
  29.3 1.8 pad_maximum_fusion
  31.1 414.1 %while.10 = (s32[]{:T(128)}, bf16[4,256,2,32]{1,3,2,0:T(8,128)(2,1)S(1)}, bf16[257,14,134]{0,2,1:T(8,128)(2,1)}, f32[4,2,7,7]{3,1,2,0:T(2,128)}, s32[]{:T(128)}) while((s32[]{:T(128)}, bf16[4,256,2,32]{1,3,2,0:T(8,128)(2,1)S(1)}, bf16[257,14,134]{0,2,1:T(8,128)(2,1)}, f32[4,2,7,7]{3,1,2,0:T(2,128)}, s32[]{:T(128)}) %tuple.29), condition=%wide.region_2.3_spmd, body=%wide.region_0.2_spmd.sunk | while | flops 312647680 | bytes 15818389 | solution.py:53
  31.1 0.7 dynamic-slice_bitcast_fusion.2
  32.0 87.6 %fusion.42 = f32[257,2,8,128]{0,1,3,2:T(2,128)S(1)} fusion(f32[2,1,7,7]{1,0,3,2:T(2,128)S(1)} %copy.40, bf16[257,1,14,134]{0,3,2,1:T(8,128)(2,1)} %bitcast.71), kind=kOutput, calls=%fused_computation.clone.1 | convolution fusion | flops 309485568 | bytes 3070000 | tf_op jit(solution)/shard_map/while/body/eval_jaxpr/conv_general_dilated | solution.py:42
  119.6 13.7 %multiply_reduce_fusion.4 = (f32[256,8,128]{0,2,1:T(8,128)S(1)}, f32[256,8,128]{0,2,1:T(8,128)S(1)}) fusion(f32[257,2,8,128]{0,1,3,2:T(2,128)S(1)} %fusion.42), kind=kLoop, calls=%fused_computation.3.clone.1 | loop fusion | flops 1835008 | bytes 6291456 | tf_op jit(solution)/shard_map/while/body/eval_jaxpr/mul | solution.py:49
  134.6 0.7 dynamic-slice_bitcast_fusion.2
  135.5 87.6 %fusion.42 = f32[257,2,8,128]{0,1,3,2:T(2,128)S(1)} fusion(f32[2,1,7,7]{1,0,3,2:T(2,128)S(1)} %copy.40, bf16[257,1,14,134]{0,3,2,1:T(8,128)(2,1)} %bitcast.71), kind=kOutput, calls=%fused_computation.clone.1 | convolution fusion | flops 309485568 | bytes 3070000 | tf_op jit(solution)/shard_map/while/body/eval_jaxpr/conv_general_dilated | solution.py:42
  223.1 13.7 %multiply_reduce_fusion.4 = (f32[256,8,128]{0,2,1:T(8,128)S(1)}, f32[256,8,128]{0,2,1:T(8,128)S(1)}) fusion(f32[257,2,8,128]{0,1,3,2:T(2,128)S(1)} %fusion.42), kind=kLoop, calls=%fused_computation.3.clone.1 | loop fusion | flops 1835008 | bytes 6291456 | tf_op jit(solution)/shard_map/while/body/eval_jaxpr/mul | solution.py:49
  238.1 0.7 dynamic-slice_bitcast_fusion.2
  239.0 87.6 %fusion.42 = f32[257,2,8,128]{0,1,3,2:T(2,128)S(1)} fusion(f32[2,1,7,7]{1,0,3,2:T(2,128)S(1)} %copy.40, bf16[257,1,14,134]{0,3,2,1:T(8,128)(2,1)} %bitcast.71), kind=kOutput, calls=%fused_computation.clone.1 | convolution fusion | flops 309485568 | bytes 3070000 | tf_op jit(solution)/shard_map/while/body/eval_jaxpr/conv_general_dilated | solution.py:42
  326.6 13.7 %multiply_reduce_fusion.4 = (f32[256,8,128]{0,2,1:T(8,128)S(1)}, f32[256,8,128]{0,2,1:T(8,128)S(1)}) fusion(f32[257,2,8,128]{0,1,3,2:T(2,128)S(1)} %fusion.42), kind=kLoop, calls=%fused_computation.3.clone.1 | loop fusion | flops 1835008 | bytes 6291456 | tf_op jit(solution)/shard_map/while/body/eval_jaxpr/mul | solution.py:49
  341.6 0.7 dynamic-slice_bitcast_fusion.2
  342.5 87.6 %fusion.42 = f32[257,2,8,128]{0,1,3,2:T(2,128)S(1)} fusion(f32[2,1,7,7]{1,0,3,2:T(2,128)S(1)} %copy.40, bf16[257,1,14,134]{0,3,2,1:T(8,128)(2,1)} %bitcast.71), kind=kOutput, calls=%fused_computation.clone.1 | convolution fusion | flops 309485568 | bytes 3070000 | tf_op jit(solution)/shard_map/while/body/eval_jaxpr/conv_general_dilated | solution.py:42
  430.1 13.7 %multiply_reduce_fusion.4 = (f32[256,8,128]{0,2,1:T(8,128)S(1)}, f32[256,8,128]{0,2,1:T(8,128)S(1)}) fusion(f32[257,2,8,128]{0,1,3,2:T(2,128)S(1)} %fusion.42), kind=kLoop, calls=%fused_computation.3.clone.1 | loop fusion | flops 1835008 | bytes 6291456 | tf_op jit(solution)/shard_map/while/body/eval_jaxpr/mul | solution.py:49
  445.2 0.9 convolution_bitcast_fusion
  446.2 89.3 %all-reduce.2.cloned.1.call-done = f32[256,256]{1,0:T(8,128)} async-done(((f32[256,256]{1,0:T(8,128)}), f32[256,256]{1,0:T(8,128)}) %all-reduce.2.cloned.1.call-update) | async-done | bytes 262160 | tf_op jit(solution)/shard_map/psum | solution.py:59
  535.5 1.3 fusion.6
  537.2 5.8 %cholesky.44 = f32[64,64]{1,0:T(8,128)S(1)} custom-call(f32[64,64]{1,0:T(8,128)S(1)} %fusion.18), custom_call_target="Cholesky" | custom-call | tf_op jit(solution)/shard_map/jit(cholesky)/cholesky | solution.py:28
  543.7 0.7 fusion.12
  544.3 4.9 custom-call.6
  549.5 1.3 fusion.4
  551.1 5.8 %cholesky.55 = f32[64,64]{1,0:T(8,128)S(1)} custom-call(f32[64,64]{1,0:T(8,128)S(1)} %fusion.16), custom_call_target="Cholesky" | custom-call | tf_op jit(solution)/shard_map/jit(cholesky)/cholesky | solution.py:28
  558.3 4.9 custom-call.7
  563.8 0.8 reshape.57
  (45 shorter events, 9.2 us)
Async XLA Ops:
  7.2 528.4 %copy-start = (f32[256,64]{0,1:T(8,128)S(1)}, f32[256,64]{0,1:T(8,128)}, u32[]{:S(2)}) copy-start(f32[256,64]{0,1:T(8,128)} %param.10) | copy-start | bytes 196612
  7.2 528.3 %all-reduce.2.cloned.1.call-start = ((), (), s32[]{:S(2)}) async-start(), calls=%async_computation | async-start | bytes 524288 | tf_op jit(solution)/shard_map/psum | solution.py:59
  8.8 8.2 %collective-permute-start = (bf16[257,3,128]{0,2,1:T(8,128)(2,1)S(1)}, bf16[257,3,128]{0,2,1:T(8,128)(2,1)S(1)}, u32[]{:S(2)}, u32[]{:S(2)}) collective-permute-start(bf16[257,3,128]{0,2,1:T(8,128)(2,1)S(1)} %get-tuple-element.39), channel_id=1, source_target_pairs={{0,4},{4,8},{8,12},{1,5},{5,9},{9,13},{2,6},{6,10},{10,14},{3,7},{... | collective-permute-start | bytes 592136 | tf_op jit(solution)/shard_map/ppermute | solution.py:20
  13.3 8.0 %collective-permute-start.1 = (bf16[257,3,128]{0,2,1:T(8,128)(2,1)S(1)}, bf16[257,3,128]{0,2,1:T(8,128)(2,1)S(1)}, u32[]{:S(2)}, u32[]{:S(2)}) collective-permute-start(bf16[257,3,128]{0,2,1:T(8,128)(2,1)S(1)} %get-tuple-element.40), channel_id=1, source_target_pairs={{4,0},{8,4},{12,8},{5,1},{9,5},{13,9},{6,2},{10,6},{14,10},{7,3},{... | collective-permute-start | bytes 592136 | tf_op jit(solution)/shard_map/ppermute | solution.py:21
  21.4 4.5 collective-permute-start.2
  24.6 4.8 collective-permute-start.3
  563.5 1.0 copy-start.1
Sparse Core Ops, SparseCore 0:
  446.3 89.1 all-reduce.1
where the time goes:
time: 572 us; the launch traced here: 571 us
  matrix products  355 us (62%)
  waiting for transfers between devices  98.9 us (17%)
  other arithmetic  83.2 us (15%)
  between operations  14.2 us (2%)
  starting transfers between devices  11 us (2%)
  local copies, waits for them, and re-layouts  8.54 us (1%)
    conv_general_dilated x4, matrix products, orient(): lax.conv_general_dilated(lifted, kernels, (1, 1), 'VALID', precision=lax....  350 us
    psum x1, waiting for transfers between devices, on_device(): gram = lax.psum(local_gram, ('row', 'col')) / npix_all  89.3 us
    mul x4, other arithmetic, orient(): prod_real * prod_real + prod_imag * prod_imag + 1.0  54.8 us
    another operation x6, other arithmetic, orthonormal(): factor = jnp.linalg.cholesky(inner)  13 us
  transfers between devices with their start and end apart: 5, of which 4 were waited for; matrix products, arithmetic and copies ran while one was open for 0% of the time, Pallas kernels for 0%

commit v1 on v0

--- a/solution.py
+++ b/solution.py
@@ -8,6 +8,11 @@
 ORIENT = 4
 TAPS = 7
 SWEEPS = 2
+
+
+def axis_by_axis(value, one, other):
+    half = lax.psum(value, one)
+    return lax.psum(half, other)
 
 
 def padded_2(array, sides, width):
@@ -56,7 +61,7 @@
     npix_all = flat.shape[1] * devices_all
     basis_now = start_basis
     local_gram = jnp.dot(flat, flat.T, preferred_element_type=jnp.float32)
-    gram = lax.psum(local_gram, ("row", "col")) / npix_all
+    gram = axis_by_axis(local_gram, "col", "row") / npix_all
     for sweep in range(SWEEPS):
         basis_now = orthonormal(jnp.dot(gram, basis_now, precision=lax.Precision.HIGHEST))
     projected = jnp.dot(basis_now.astype(jnp.bfloat16).T, flat, preferred_element_type=jnp.float32)

time: 572 us -> 552 us (0.965)
  waiting for transfers between devices: 98.9 us -> 77.2 us
    psum x1 -> x2, waiting for transfers between devices: 89.3 us -> 67.6 us  [the longest x1 34 us: axis_by_axis(): return lax.psum(half, other)]
  transfers between devices with their start and end apart: 5 -> 6, of which waited for: 4 -> 5; matrix products, arithmetic and copies ran while one was open for 0% -> 0% of each run, Pallas kernels for 0% -> 0%
where the time goes in v1:
time: 552 us; the launch traced here: 550 us
  matrix products  355 us (64%)
  other arithmetic  83.2 us (15%)
  waiting for transfers between devices  77.2 us (14%)
  between operations  14.2 us (3%)
  starting transfers between devices  11.2 us (2%)
  local copies, waits for them, and re-layouts  8.53 us (2%)
    conv_general_dilated x4, matrix products, orient(): lax.conv_general_dilated(lifted, kernels, (1, 1), 'VALID', precision=lax....  350 us
    mul x4, other arithmetic, orient(): prod_real * prod_real + prod_imag * prod_imag + 1.0  54.8 us
    psum x1, waiting for transfers between devices, axis_by_axis(): return lax.psum(half, other)  34 us
    psum x1, waiting for transfers between devices, axis_by_axis(): half = lax.psum(value, one)  33.6 us
    another operation x6, other arithmetic, orthonormal(): factor = jnp.linalg.cholesky(inner)  13 us
    another operation x4, other arithmetic, orthonormal(): lax.linalg.triangular_solve(factor, stacked, left_side=False, lower=True,...  11.1 us
  transfers between devices with their start and end apart: 6, of which 5 were waited for; matrix products, arithmetic and copies ran while one was open for 0% of the time, Pallas kernels for 0%

profile of v1, /device:TPU:1, one launch (start us, length us, event | category | flops | bytes accessed | tf_op | source)
XLA Modules:
  0.0 549.7 jit_solution(4677316902731328907)
XLA Ops:
  7.2 1.5 copy.25
  8.8 4.5 collective-permute-start
  13.3 1.9 collective-permute-start.1
  15.2 1.7 collective-permute-done
  16.9 4.4 collective-permute-done.1
  21.4 3.2 collective-permute-start.2
  24.6 1.3 collective-permute-start.3
  25.9 3.4 collective-permute-done.3
  29.3 1.8 pad_maximum_fusion
  31.1 413.9 %while.10 = (s32[]{:T(128)}, bf16[4,256,2,32]{1,3,2,0:T(8,128)(2,1)S(1)}, bf16[257,14,134]{0,2,1:T(8,128)(2,1)}, f32[4,2,7,7]{3,1,2,0:T(2,128)}, s32[]{:T(128)}) while((s32[]{:T(128)}, bf16[4,256,2,32]{1,3,2,0:T(8,128)(2,1)S(1)}, bf16[257,14,134]{0,2,1:T(8,128)(2,1)}, f32[4,2,7,7]{3,1,2,0:T(2,128)}, s32[]{:T(128)}) %tuple.29), condition=%wide.region_2.3_spmd, body=%wide.region_0.2_spmd.sunk | while | flops 312647680 | bytes 15818389 | solution.py:58
  31.1 0.7 dynamic-slice_bitcast_fusion.2
  32.0 87.6 %fusion.42 = f32[257,2,8,128]{0,1,3,2:T(2,128)S(1)} fusion(f32[2,1,7,7]{1,0,3,2:T(2,128)S(1)} %copy.40, bf16[257,1,14,134]{0,3,2,1:T(8,128)(2,1)} %bitcast.71), kind=kOutput, calls=%fused_computation.clone.1 | convolution fusion | flops 309485568 | bytes 3070000 | tf_op jit(solution)/shard_map/while/body/eval_jaxpr/conv_general_dilated | solution.py:47
  119.6 13.7 %multiply_reduce_fusion.4 = (f32[256,8,128]{0,2,1:T(8,128)S(1)}, f32[256,8,128]{0,2,1:T(8,128)S(1)}) fusion(f32[257,2,8,128]{0,1,3,2:T(2,128)S(1)} %fusion.42), kind=kLoop, calls=%fused_computation.3.clone.1 | loop fusion | flops 1835008 | bytes 6291456 | tf_op jit(solution)/shard_map/while/body/eval_jaxpr/mul | solution.py:54
  134.6 0.7 dynamic-slice_bitcast_fusion.2
  135.5 87.6 %fusion.42 = f32[257,2,8,128]{0,1,3,2:T(2,128)S(1)} fusion(f32[2,1,7,7]{1,0,3,2:T(2,128)S(1)} %copy.40, bf16[257,1,14,134]{0,3,2,1:T(8,128)(2,1)} %bitcast.71), kind=kOutput, calls=%fused_computation.clone.1 | convolution fusion | flops 309485568 | bytes 3070000 | tf_op jit(solution)/shard_map/while/body/eval_jaxpr/conv_general_dilated | solution.py:47
  223.1 13.7 %multiply_reduce_fusion.4 = (f32[256,8,128]{0,2,1:T(8,128)S(1)}, f32[256,8,128]{0,2,1:T(8,128)S(1)}) fusion(f32[257,2,8,128]{0,1,3,2:T(2,128)S(1)} %fusion.42), kind=kLoop, calls=%fused_computation.3.clone.1 | loop fusion | flops 1835008 | bytes 6291456 | tf_op jit(solution)/shard_map/while/body/eval_jaxpr/mul | solution.py:54
  238.1 0.7 dynamic-slice_bitcast_fusion.2
  239.0 87.6 %fusion.42 = f32[257,2,8,128]{0,1,3,2:T(2,128)S(1)} fusion(f32[2,1,7,7]{1,0,3,2:T(2,128)S(1)} %copy.40, bf16[257,1,14,134]{0,3,2,1:T(8,128)(2,1)} %bitcast.71), kind=kOutput, calls=%fused_computation.clone.1 | convolution fusion | flops 309485568 | bytes 3070000 | tf_op jit(solution)/shard_map/while/body/eval_jaxpr/conv_general_dilated | solution.py:47
  326.6 13.7 %multiply_reduce_fusion.4 = (f32[256,8,128]{0,2,1:T(8,128)S(1)}, f32[256,8,128]{0,2,1:T(8,128)S(1)}) fusion(f32[257,2,8,128]{0,1,3,2:T(2,128)S(1)} %fusion.42), kind=kLoop, calls=%fused_computation.3.clone.1 | loop fusion | flops 1835008 | bytes 6291456 | tf_op jit(solution)/shard_map/while/body/eval_jaxpr/mul | solution.py:54
  341.6 0.7 dynamic-slice_bitcast_fusion.2
  342.5 87.6 %fusion.42 = f32[257,2,8,128]{0,1,3,2:T(2,128)S(1)} fusion(f32[2,1,7,7]{1,0,3,2:T(2,128)S(1)} %copy.40, bf16[257,1,14,134]{0,3,2,1:T(8,128)(2,1)} %bitcast.71), kind=kOutput, calls=%fused_computation.clone.1 | convolution fusion | flops 309485568 | bytes 3070000 | tf_op jit(solution)/shard_map/while/body/eval_jaxpr/conv_general_dilated | solution.py:47
  430.1 13.7 %multiply_reduce_fusion.4 = (f32[256,8,128]{0,2,1:T(8,128)S(1)}, f32[256,8,128]{0,2,1:T(8,128)S(1)}) fusion(f32[257,2,8,128]{0,1,3,2:T(2,128)S(1)} %fusion.42), kind=kLoop, calls=%fused_computation.3.clone.1 | loop fusion | flops 1835008 | bytes 6291456 | tf_op jit(solution)/shard_map/while/body/eval_jaxpr/mul | solution.py:54
  445.1 0.9 convolution_bitcast_fusion
  446.2 33.6 %all-reduce.3.cloned.1.call-done = f32[256,256]{1,0:T(8,128)} async-done(((f32[256,256]{1,0:T(8,128)}), f32[256,256]{1,0:T(8,128)}) %all-reduce.3.cloned.1.call-update) | async-done | bytes 262160 | tf_op jit(solution)/shard_map/psum | solution.py:14
  479.8 34.0 %all-reduce.5.cloned.1.call-done = f32[256,256]{1,0:T(8,128)} async-done(((f32[256,256]{1,0:T(8,128)}), f32[256,256]{1,0:T(8,128)}) %all-reduce.5.cloned.1.call-update) | async-done | bytes 262160 | tf_op jit(solution)/shard_map/psum | solution.py:15
  513.9 1.3 fusion.6
  515.5 5.8 %cholesky.44 = f32[64,64]{1,0:T(8,128)S(1)} custom-call(f32[64,64]{1,0:T(8,128)S(1)} %fusion.18), custom_call_target="Cholesky" | custom-call | tf_op jit(solution)/shard_map/jit(cholesky)/cholesky | solution.py:33
  522.7 4.9 custom-call.6
  527.8 1.3 fusion.4
  529.5 5.8 %cholesky.55 = f32[64,64]{1,0:T(8,128)S(1)} custom-call(f32[64,64]{1,0:T(8,128)S(1)} %fusion.16), custom_call_target="Cholesky" | custom-call | tf_op jit(solution)/shard_map/jit(cholesky)/cholesky | solution.py:33
  536.7 4.9 custom-call.7
  542.1 0.8 reshape.57
  (48 shorter events, 10.1 us)
Async XLA Ops:
  7.2 506.7 %copy-start = (f32[256,64]{0,1:T(8,128)S(1)}, f32[256,64]{0,1:T(8,128)}, u32[]{:S(2)}) copy-start(f32[256,64]{0,1:T(8,128)} %param.10) | copy-start | bytes 196612
  7.2 472.6 %all-reduce.3.cloned.1.call-start = ((), (), s32[]{:S(2)}) async-start(), calls=%async_computation | async-start | bytes 524288 | tf_op jit(solution)/shard_map/psum | solution.py:14
  8.8 8.2 %collective-permute-start = (bf16[257,3,128]{0,2,1:T(8,128)(2,1)S(1)}, bf16[257,3,128]{0,2,1:T(8,128)(2,1)S(1)}, u32[]{:S(2)}, u32[]{:S(2)}) collective-permute-start(bf16[257,3,128]{0,2,1:T(8,128)(2,1)S(1)} %get-tuple-element.39), channel_id=1, source_target_pairs={{0,4},{4,8},{8,12},{1,5},{5,9},{9,13},{2,6},{6,10},{10,14},{3,7},{... | collective-permute-start | bytes 592136 | tf_op jit(solution)/shard_map/ppermute | solution.py:25
  13.3 8.0 %collective-permute-start.1 = (bf16[257,3,128]{0,2,1:T(8,128)(2,1)S(1)}, bf16[257,3,128]{0,2,1:T(8,128)(2,1)S(1)}, u32[]{:S(2)}, u32[]{:S(2)}) collective-permute-start(bf16[257,3,128]{0,2,1:T(8,128)(2,1)S(1)} %get-tuple-element.40), channel_id=1, source_target_pairs={{4,0},{8,4},{12,8},{5,1},{9,5},{13,9},{6,2},{10,6},{14,10},{7,3},{... | collective-permute-start | bytes 592136 | tf_op jit(solution)/shard_map/ppermute | solution.py:26
  21.4 4.5 collective-permute-start.2
  24.6 4.8 collective-permute-start.3
  446.0 67.8 %all-reduce.5.cloned.1.call-start = ((), (), s32[]{:S(2)}) async-start(), calls=%async_computation.1 | async-start | bytes 524288 | tf_op jit(solution)/shard_map/psum | solution.py:15
  541.8 1.0 copy-start.1
Sparse Core Ops, SparseCore 0:
  446.1 33.6 all-reduce.2
  482.2 31.5 all-reduce.4
